TPU v7x, 128 devices: a whole 4x4x4 slice. The times are simulated.
128 devices in a mesh: dom: 32 (over y, z, core), sub: 4 (over x).
Axes of the slice: x: 4, y: 4, z: 4, core: 2. Of those that a mesh axis runs over, the one named last changes fastest.
Arguments:
- displace: float32 [3, 262144, 128], P(None, ('dom', 'sub')), may hold values from -3 to 3
- velocity: float32 [3, 262144, 128], P(None, ('dom', 'sub')), may hold values from -3 to 3
- nodal_mass: float32 [262144, 128], P(('dom', 'sub')), may hold values from 1 to 4
- stiffness: float32 [262144, 128], P(('dom', 'sub')), may hold values from 0.5 to 2
- die_planes: float32 [3, 8192, 4, 128], P(None, ('dom', 'sub')), may hold values from -3 to 3
- owners: int32 [3, 16384, 1], P(None, ('dom', 'sub')), may hold values from 0 to 127; in each aligned block of 128 rows (0 to 127, 128 to 255, ..., all dimensions but the last counted through in order) at most 2 rows name the same one
- pairs: int32 [3, 16384], P(None, ('dom', 'sub')), may hold values from 0 to 63
Outputs:
- final_displace: float32 [3, 262144, 128], P(None, ('dom', 'sub'))
- final_velocity: float32 [3, 262144, 128], P(None, ('dom', 'sub'))
Inputs may be any that keep to these rules, and one draw needn't show every extreme that they name: `owners`: in each step, no bin owner gets more than 2 of the segment blocks of one device, and some device sends exactly 2 to one owner.
All inputs are finite; a program needn't handle non-finite values.
Results may differ from a plain program's by a relative error of at most 0.0001.
Values sent between devices are 32-bit elements; how exact they have to be, the bound alone decides.
A program may use at most 128 MiB of HBM per device.

v0:
```python
import functools

import jax
import jax.numpy as jnp
from jax import lax
from jax.experimental import pallas as pl
from jax.experimental.pallas import tpu as pltpu
from jax.sharding import PartitionSpec as P

STEPS = 3
time_step = 0.2
penalty = 1.0

MESH = pl.DeviceIdType.MESH
PAD = 16
HALO = 8


def next_col(x):
    return pltpu.roll(x, x.shape[-1] - 1, x.ndim - 1)


def prev_col(x):
    return pltpu.roll(x, 1, x.ndim - 1)


def contact(planes, position):
    normal, height = planes[:3], planes[3]
    depth = height - (normal[0] * position[0] + normal[1] * position[1] + normal[2] * position[2])
    push = penalty * jnp.maximum(depth, 0.0)
    return [push * normal[c] for c in range(3)]


def contact_response(planes, rows):
    cm = {o: rows("cm", o) for o in range(-2, 3)}
    kq = {o: rows("kq", o) for o in range(-2, 2)}
    w4 = {o: rows("w4", o) for o in range(-1, 2)}
    u = {}
    z = {}
    for step in range(STEPS):
        free = rows("d%d" % step, 0)
        position = [free[c] + u[0][c] if step else free[c] for c in range(3)]
        push = contact(planes[step], position)
        new_u, new_z = {}, {}
        for o in range(-step, step + 1):
            new_u[o], new_z[o] = [], []
        for c in range(3):
            spread = {}
            for o in range(-step, step):
                parts = [u[r][c] for r in (o, o + 1) if r in u]
                box = parts[0] if len(parts) == 1 else parts[0] + parts[1]
                t = kq[o] * (box + next_col(box))
                spread[o] = t + prev_col(t)
            for o in range(-step, step + 1):
                terms = [spread[r] for r in (o - 1, o) if r in spread]
                if o in u:
                    terms.append(-(w4[o] * u[o][c]))
                if o == 0:
                    terms.append(push[c])
                force = terms[0]
                for term in terms[1:]:
                    force = force + term
                dz = cm[o] * force
                zc = z[o][c] + dz if o in z else dz
                uc = time_step * zc
                if o in u:
                    uc = u[o][c] + uc
                new_z[o].append(zc)
                new_u[o].append(uc)
        u, z = new_u, new_z
    return u, z


def kernel(
    n_dom, n_sub, cap, near, block, last_block, width,
    own_hbm, pair_hbm, d_hbm, v_hbm, m_hbm, k_hbm, die_hbm,
    od_ref, ov_ref,
    own_ref, pair_ref, d0, d1, d2, vel, cm, kq, w4, die, req, passed, asked, asked_rows, asked_s, idx, idx_s, answer, got, planes, first_patch, ghost, above_u, above_z,
    load_sem, halo_send, halo_recv, req_send, req_recv, ans_send, ans_recv, small_sem, ghost_sem,
):
    n = n_dom * n_sub
    steps, seg = pair_hbm.shape
    here = d_hbm.shape[1]
    stride = here // seg
    ncol = d_hbm.shape[2]
    slots = steps * cap
    lists_rows = asked_s.shape[0]
    patches = die_hbm.shape[1]
    dom, sub = lax.axis_index("dom"), lax.axis_index("sub")
    me = dom * n_sub + sub

    def device(i):
        return (lax.div(i, n_sub), lax.rem(i, n_sub))

    far = n // near
    my_w = lax.rem(dom, near)
    my_g = lax.div(dom, near) * n_sub + sub

    def device_at(g, w):
        return (lax.div(g, n_sub) * near + w, lax.rem(g, n_sub))

    def other_group(t):
        return lax.rem(my_g + t, far)

    def other_member(t):
        return lax.rem(my_w + t, near)

    def partner(t):
        return lax.rem(me + t * 37, n)

    following, previous = lax.rem(me + 1, n), lax.rem(me + n - 1, n)

    inner = pl.ds(PAD, here)
    lists = [
        pltpu.make_async_copy(own_hbm, own_ref, load_sem.at[5]),
        pltpu.make_async_copy(pair_hbm, pair_ref, load_sem.at[6]),
    ]
    loads = [
        pltpu.make_async_copy(d_hbm, d0.at[:, inner], load_sem.at[0]),
        pltpu.make_async_copy(v_hbm, vel.at[:, inner], load_sem.at[1]),
        pltpu.make_async_copy(m_hbm, cm.at[inner], load_sem.at[2]),
        pltpu.make_async_copy(k_hbm, kq.at[inner], load_sem.at[3]),
        pltpu.make_async_copy(die_hbm, die, load_sem.at[4]),
    ]
    for copy in lists + loads:
        copy.start()

    barrier = pltpu.get_barrier_semaphore()

    def greet(to):
        pl.semaphore_signal(barrier, inc=1, device_id=to, device_id_type=MESH)

    def greet_groups(t, carry):
        greet(device_at(other_group(t), my_w))
        return carry

    def greet_members(t, carry):
        greet(device_at(my_g, other_member(t)))
        return carry

    lax.fori_loop(1, far, greet_groups, 0)
    lax.fori_loop(1, near, greet_members, 0)
    greet(device(following))
    greet(device(previous))

    lane_of = lax.broadcasted_iota(jnp.int32, (n, 128), 1)
    row = lax.broadcasted_iota(jnp.int32, (n, seg), 0)
    row_g, row_w = lax.div(row, near), lax.rem(row, near)
    owner_of = (lax.div(row_g, n_sub) * near + row_w) * n_sub + lax.rem(row_g, n_sub)
    before = lax.broadcasted_iota(jnp.int32, (seg, seg), 0) < lax.broadcasted_iota(jnp.int32, (seg, seg), 1)
    table = jnp.zeros((n, 128), jnp.int32)
    places = []
    for copy in lists:
        copy.wait()
    for s in range(steps):
        own = own_ref[s]
        wide = jnp.broadcast_to(own, (seg, seg))
        same = (wide == wide.T) & before
        slot = jnp.minimum(jnp.sum(same.astype(jnp.int32), axis=0, keepdims=True), cap - 1)
        places.append(own * slots + (s * cap + slot))
        pair = pair_ref[s : s + 1, :]
        mine = owner_of == own
        for k in range(cap):
            chosen = jnp.where(mine & (slot == k), pair, 0)
            table = jnp.where(lane_of == s * cap + k, jnp.sum(chosen, axis=1, keepdims=True), table)
    req[...] = table.reshape(far, near, 128)
    pl.semaphore_wait(barrier, far + near)

    def ask(t, carry):
        g = other_group(t)
        pltpu.make_async_remote_copy(
            req.at[g], passed.at[my_g], req_send.at[0], req_recv.at[0],
            device_id=device_at(g, my_w), device_id_type=MESH,
        ).start()
        return carry

    lax.fori_loop(1, far, ask, 0)
    pltpu.make_async_copy(req.at[my_g], passed.at[my_g], req_recv.at[0]).start()

    for s in range(steps):
        idx[s : s + 1, :] = places[s]
    idx_copy = pltpu.make_async_copy(idx, idx_s, small_sem.at[0])
    idx_copy.start()

    first, last = pl.ds(0, HALO), pl.ds(here - HALO, HALO)
    front, back = pl.ds(PAD - HALO, HALO), pl.ds(PAD + here, HALO)
    halos = []
    for a, (src, dst) in enumerate(((d_hbm, d0), (v_hbm, vel), (m_hbm, cm), (k_hbm, kq))):
        three = len(src.shape) == 3
        for side, (rows, place, to) in enumerate(((last, front, following), (first, back, previous))):
            copy = pltpu.make_async_remote_copy(
                src.at[:, rows] if three else src.at[rows],
                dst.at[:, place] if three else dst.at[place],
                halo_send.at[2 * a + side], halo_recv.at[2 * a + side],
                device_id=device(to), device_id_type=MESH,
            )
            copy.start()
            halos.append(copy)

    for copy in loads:
        copy.wait()

    def prepare(base, size):
        at = pl.ds(base, size)
        col = lax.broadcasted_iota(jnp.int32, (size, ncol), 1)
        kq[at, :] = jnp.where(col < ncol - 1, kq[at, :] * 0.25, 0.0)
        cm[at, :] = time_step / cm[at, :]

    def prepare_block(b, carry):
        prepare(pl.multiple_of(PAD + b * last_block, 8), last_block)
        return carry

    lax.fori_loop(0, here // last_block, prepare_block, 0)

    pltpu.make_async_copy(req, passed, req_recv.at[0]).wait()

    def hand_on(t, carry):
        w = other_member(t)
        pltpu.make_async_remote_copy(
            passed.at[:, w], asked.at[my_w], req_send.at[1], req_recv.at[1],
            device_id=device_at(my_g, w), device_id_type=MESH,
        ).start()
        return carry

    lax.fori_loop(1, near, hand_on, 0)
    pltpu.make_async_copy(passed.at[:, my_w], asked.at[my_w], req_recv.at[1]).start()

    for copy in halos:
        copy.wait()
    prepare(PAD - HALO, HALO)
    prepare(PAD + here, HALO)

    @pl.when(me == 0)
    def _():
        kq[front, :] = jnp.zeros((HALO, ncol), jnp.float32)

    @pl.when(me == n - 1)
    def _():
        tail = pl.ds(PAD + here - HALO, HALO)
        row = lax.broadcasted_iota(jnp.int32, (HALO, ncol), 0)
        kq[tail, :] = jnp.where(row == HALO - 1, 0.0, kq[tail, :])

    blocks = (here + 2 * HALO) // block
    assert blocks * block == here + 2 * HALO

    def weights(b, carry):
        base = pl.multiple_of(PAD - HALO + b * block, 8)
        both = kq[pl.ds(base, block), :] + kq[pl.ds(base - 1, block), :]
        w4[pl.ds(base, block), :] = 4.0 * (both + prev_col(both))
        return carry

    lax.fori_loop(0, blocks, weights, 0)

    pltpu.make_async_copy(asked, asked, req_recv.at[1]).wait()
    asked_rows[...] = asked[...].reshape(n, 128).T[:lists_rows]
    to_scalar = pltpu.make_async_copy(asked_rows, asked_s, small_sem.at[1])
    to_scalar.start()
    to_scalar.wait()
    idx_copy.wait()

    def gather(p, dst, at):
        p_dom, p_sub = device(p)
        w, g = lax.rem(p_dom, near), lax.div(p_dom, near) * n_sub + p_sub
        for s in range(steps):
            for k in range(cap):
                dst[at + (s * cap + k)] = die[s, jnp.clip(asked_s[s * cap + k, w * far + g], 0, patches - 1)]

    def reply(t, carry):
        p = partner(t)
        gather(p, answer, p * slots)
        pltpu.make_async_remote_copy(
            answer.at[pl.ds(p * slots, slots)], got.at[pl.ds(me * slots, slots)], ans_send, ans_recv,
            device_id=device(p), device_id_type=MESH,
        ).start()
        return carry

    lax.fori_loop(1, n, reply, 0)
    gather(me, got, me * slots)

    def free_step(src, d_to, v_to, first_row, count, size):
        def part(b, carry):
            base = pl.multiple_of(first_row + b * size, 8)
            top_row = lax.broadcasted_iota(jnp.int32, (8, ncol), 0) == 0
            shifted = [None] * 3
            for i in range(size // 8 + 1):
                at = pl.ds(base + 8 * (i - 1), 8)
                below = pl.ds(base + 8 * (i - 1) + 1, 8)
                for c in range(3):
                    d = src[c, at, :]
                    box = d + src[c, below, :]
                    t = kq[at, :] * (box + next_col(box))
                    down = pltpu.roll(t, 1, 0)
                    if i:
                        t = t + jnp.where(top_row, shifted[c], down)
                        force = t + prev_col(t) - w4[at, :] * d
                        v = vel[c, at, :] + cm[at, :] * force
                        v_to(base, size)[c, 8 * (i - 1) : 8 * i, :] = v
                        d_to(base, size)[c, 8 * (i - 1) : 8 * i, :] = d + time_step * v
                    shifted[c] = down
            return carry

        lax.fori_loop(0, count, part, 0)

    def same_rows(ref):
        return lambda base, size: ref.at[:, pl.ds(base, size)]

    def own_rows(ref):
        return lambda base, size: ref.at[:, pl.ds(pl.multiple_of(base - PAD, 8), size)]

    free_step(d0, same_rows(d1), same_rows(vel), PAD - HALO, blocks, block)
    free_step(d1, same_rows(d2), same_rows(vel), PAD - HALO, blocks, block)
    free_step(d2, own_rows(od_ref), own_rows(ov_ref), PAD, here // last_block, last_block)

    wire = pl.ds(0, (n - 1) * slots)
    pltpu.make_async_copy(answer.at[wire], got.at[wire], ans_recv).wait()

    for s in range(steps):
        first_patch[s] = got[idx_s[s, 0]]
    ghost_copy = pltpu.make_async_remote_copy(
        first_patch, ghost, ghost_sem.at[0], ghost_sem.at[1],
        device_id=device(previous), device_id_type=MESH,
    )
    ghost_copy.start()

    def place(j, carry):
        for s in range(steps):
            planes[s, pl.ds(j * 4, 4), :] = got[idx_s[s, j]]
        return carry

    lax.fori_loop(0, seg, place, 0, unroll=8)

    flat = {"cm": cm, "kq": kq, "w4": w4}
    deep = {"d0": d0, "d1": d1, "d2": d2}
    chunk = width * stride

    def correct(q, carry):
        base = PAD + q * chunk

        def rows(name, o):
            at = pl.ds(base + o, width, stride=stride)
            if name in flat:
                return flat[name][at, :]
            return [deep[name][c, at, :] for c in range(3)]

        nearby = [[planes[s, pl.ds(q * width * 4 + c, width, stride=4), :] for c in range(4)] for s in range(steps)]
        u, z = contact_response(nearby, rows)
        for c in range(3):
            for o in range(0, 3):
                at = pl.ds(q * chunk + o, width, stride=stride)
                od_ref[c, at, :] += u[o][c]
                ov_ref[c, at, :] += z[o][c]
            for o in (-2, -1):
                at = pl.ds(pl.multiple_of(q * width, 8), width)
                above_u[o + 2, c, at, :] = u[o][c]
                above_z[o + 2, c, at, :] = z[o][c]
        return carry

    lax.fori_loop(0, seg // width, correct, 0)

    ghost_copy.wait()

    def ghost_rows(name, o):
        at = pl.ds(PAD + here + o, 1)
        if name in flat:
            return flat[name][at, :]
        return [deep[name][c, at, :] for c in range(3)]

    nearby = [[ghost[s, pl.ds(c, 1), :] for c in range(4)] for s in range(steps)]
    u, z = contact_response(nearby, ghost_rows)
    for o in (-2, -1):
        for c in range(3):
            above_u[o + 2, c, pl.ds(seg, 1), :] = u[o][c]
            above_z[o + 2, c, pl.ds(seg, 1), :] = z[o][c]

    def correct_above(q, carry):
        for o in (-2, -1):
            at = pl.ds(q * chunk + stride + o, width, stride=stride)
            block_after = pl.ds(q * width + 1, width)
            for c in range(3):
                od_ref[c, at, :] += above_u[o + 2, c, block_after, :]
                ov_ref[c, at, :] += above_z[o + 2, c, block_after, :]
        return carry

    lax.fori_loop(0, seg // width, correct_above, 0)

    pltpu.make_async_copy(answer.at[wire], got.at[wire], ans_send).wait()
    pltpu.make_async_copy(req.at[pl.ds(0, far - 1)], passed.at[pl.ds(0, far - 1)], req_send.at[0]).wait()
    pltpu.make_async_copy(asked.at[pl.ds(0, near - 1)], asked.at[pl.ds(0, near - 1)], req_send.at[1]).wait()


def body(n_dom, n_sub, displace, velocity, nodal_mass, stiffness, die_planes, owners, pairs):
    n = n_dom * n_sub
    here, ncol = displace.shape[1:]
    steps, seg = pairs.shape
    cap = max(2, 2 * seg // n)
    slots = steps * cap
    ext = here + 2 * PAD
    tiles = (here + 2 * HALO) // 8
    block = 8 * max(b for b in range(1, 44) if tiles % b == 0)
    last_block = 8 * max(b for b in range(1, 33) if here // 8 % b == 0)
    width = min(32, seg)
    near = min(8, n_dom // 2)
    far = n // near
    f32, i32 = jnp.float32, jnp.int32
    any_spec = pl.BlockSpec(memory_space=pl.ANY)
    vmem_spec = pl.BlockSpec(memory_space=pltpu.VMEM)
    dma = pltpu.SemaphoreType.DMA
    return pl.pallas_call(
        functools.partial(kernel, n_dom, n_sub, cap, near, block, last_block, width),
        out_shape=[pltpu.VMEM(displace.shape, f32)] * 2,
        in_specs=[any_spec] * 7,
        out_specs=[vmem_spec] * 2,
        scratch_shapes=[
            pltpu.VMEM((steps, 1, seg), i32),
            pltpu.VMEM((steps, seg), i32),
            pltpu.VMEM((3, ext, ncol), f32),
            pltpu.VMEM((3, ext, ncol), f32),
            pltpu.VMEM((3, ext, ncol), f32),
            pltpu.VMEM((3, ext, ncol), f32),
            pltpu.VMEM((ext, ncol), f32),
            pltpu.VMEM((ext, ncol), f32),
            pltpu.VMEM((ext, ncol), f32),
            pltpu.VMEM(die_planes.shape, f32),
            pltpu.VMEM((far, near, 128), i32),
            pltpu.VMEM((far, near, 128), i32),
            pltpu.VMEM((near, far, 128), i32),
            pltpu.VMEM((-(-slots // 8) * 8, n), i32),
            pltpu.SMEM((-(-slots // 8) * 8, n), i32),
            pltpu.VMEM((8, seg), i32),
            pltpu.SMEM((8, seg), i32),
            pltpu.VMEM((n * slots, 4, ncol), f32),
            pltpu.VMEM((n * slots, 4, ncol), f32),
            pltpu.VMEM((steps, seg * 4 + 32, ncol), f32),
            pltpu.VMEM((steps, 4, ncol), f32),
            pltpu.VMEM((steps, 4, ncol), f32),
            pltpu.VMEM((2, 3, seg + 8, ncol), f32),
            pltpu.VMEM((2, 3, seg + 8, ncol), f32),
            dma((7,)), dma((8,)), dma((8,)), dma((2,)), dma((2,)), dma, dma, dma((2,)), dma((2,)),
        ],
        compiler_params=pltpu.CompilerParams(
            collective_id=0, has_side_effects=True, vmem_limit_bytes=40 * 1024 * 1024
        ),
        name="stamp",
    )(*[
        pltpu.with_memory_space_constraint(x, pltpu.HBM)
        for x in (jnp.swapaxes(owners, 1, 2), pairs, displace, velocity, nodal_mass, stiffness, die_planes)
    ])


def solution(mesh):
    in_specs = (
        P(None, ("dom", "sub"), None),
        P(None, ("dom", "sub"), None),
        P(("dom", "sub"), None),
        P(("dom", "sub"), None),
        P(None, ("dom", "sub"), None, None),
        P(None, ("dom", "sub"), None),
        P(None, ("dom", "sub")),
    )
    out_specs = (P(None, ("dom", "sub"), None), P(None, ("dom", "sub"), None))
    run = functools.partial(body, mesh.shape["dom"], mesh.shape["sub"])
    return jax.shard_map(run, mesh=mesh, in_specs=in_specs, out_specs=out_specs, check_vma=False)
```

profile of v0, /device:TPU:1, one launch (start us, length us, event | category | flops | bytes accessed | tf_op | source)
XLA Modules:
  0.0 47.6 jit_solution(3016711269469579672)
XLA Ops:
  0.6 43.6 %stamp.1 = (f32[3,2048,128]{2,1,0:T(8,128)S(1)}, f32[3,2048,128]{2,1,0:T(8,128)S(1)}) custom-call(s32[3,1,128]{2,1,0:T(1,128)} %bitcast.1, s32[3,128]{1,0:T(4,128)} %pair_hbm.1, f32[3,2048,128]{2,1,0:T(8,128)} %d_hbm.1, f32[3,2048,128]{2,1,0:T(8,128)} %v_hbm.1, f32[2048,128]{1,0:T(8,128)} %m_hbm.1, f32[2048,128]{1,0:T(8,128)} %k_hbm.1, f32[3,64,4,128]{3,2,1,0:T(4,128)} %die_hbm.1), custom_call_target="tpu_custom_call" | custom-call | tf_op jit(solution)/shard_map/stamp/pallas_call | solution.py:408
  44.3 1.7 %copy.11 = f32[3,2048,128]{2,1,0:T(8,128)} copy(f32[3,2048,128]{2,1,0:T(8,128)S(1)} %get-tuple-element.2) | data formatting | bytes 6291456
  45.9 1.7 %copy.12 = f32[3,2048,128]{2,1,0:T(8,128)} copy(f32[3,2048,128]{2,1,0:T(8,128)S(1)} %get-tuple-element.3) | data formatting | bytes 6291456
where the time goes:
time: 47.7 us; the launch traced here: 47.6 us
  Pallas kernels  43.6 us (91%)
  local copies, waits for them, and re-layouts  3.33 us (7%)
  between operations  0.64 us (1%)
    pallas_call x1, Pallas kernels, body(): pl.pallas_call(functools.partial(kernel, n_dom, n_sub, cap, near, block,...  43.6 us
    unnamed x2, local copies, waits for them, and re-layouts  3.33 us

commit v1 on v0

--- a/solution.py
+++ b/solution.py
@@ -14,6 +14,7 @@
 MESH = pl.DeviceIdType.MESH
 PAD = 16
 HALO = 8
+LEAD = 2
 
 
 def next_col(x):
@@ -72,7 +73,7 @@
 
 
 def kernel(
-    n_dom, n_sub, cap, near, block, last_block, width,
+    n_dom, n_sub, cap, near, lead, block, last_block, width,
     own_hbm, pair_hbm, d_hbm, v_hbm, m_hbm, k_hbm, die_hbm,
     od_ref, ov_ref,
     own_ref, pair_ref, d0, d1, d2, vel, cm, kq, w4, die, req, passed, asked, asked_rows, asked_s, idx, idx_s, answer, got, planes, first_patch, ghost, above_u, above_z,
@@ -104,9 +105,6 @@
 
     def other_member(t):
         return lax.rem(my_w + t, near)
-
-    def partner(t):
-        return lax.rem(me + t * 37, n)
 
     following, previous = lax.rem(me + 1, n), lax.rem(me + n - 1, n)
 
@@ -258,24 +256,40 @@
     to_scalar.wait()
     idx_copy.wait()
 
-    def gather(p, dst, at):
-        p_dom, p_sub = device(p)
-        w, g = lax.rem(p_dom, near), lax.div(p_dom, near) * n_sub + p_sub
+    def gather(w, g, dst, at):
         for s in range(steps):
             for k in range(cap):
                 dst[at + (s * cap + k)] = die[s, jnp.clip(asked_s[s * cap + k, w * far + g], 0, patches - 1)]
 
-    def reply(t, carry):
-        p = partner(t)
-        gather(p, answer, p * slots)
-        pltpu.make_async_remote_copy(
-            answer.at[pl.ds(p * slots, slots)], got.at[pl.ds(me * slots, slots)], ans_send, ans_recv,
-            device_id=device(p), device_id_type=MESH,
-        ).start()
-        return carry
-
-    lax.fori_loop(1, n, reply, 0)
-    gather(me, got, me * slots)
+    layers = max(1, near // 2)
+    cores = near // layers
+    per_layer = n // layers
+    my_layer, my_core = lax.div(my_w, cores), lax.rem(my_w, cores)
+    my_place = (lax.div(my_g, n_sub) * cores + my_core) * n_sub + sub
+
+    def reply(layer, turn):
+        place = lax.rem(my_place + turn * 13, per_layer)
+        line, x = lax.div(place, n_sub), lax.rem(place, n_sub)
+        w = layer * cores + lax.rem(line, cores)
+        g = lax.div(line, cores) * n_sub + x
+        to = device_at(g, w)
+        p = to[0] * n_sub + to[1]
+
+        @pl.when((turn >= 0) & (turn < per_layer) & (p != me))
+        def _():
+            gather(w, g, answer, p * slots)
+            pltpu.make_async_remote_copy(
+                answer.at[pl.ds(p * slots, slots)], got.at[pl.ds(me * slots, slots)], ans_send, ans_recv,
+                device_id=to, device_id_type=MESH,
+            ).start()
+
+    def reply_round(i, carry):
+        for layer in range(layers):
+            reply(layer, i - lead * layer)
+        return carry
+
+    lax.fori_loop(0, per_layer + lead * (layers - 1), reply_round, 0)
+    gather(my_w, my_g, got, me * slots)
 
     def free_step(src, d_to, v_to, first_row, count, size):
         def part(b, carry):
@@ -406,7 +420,7 @@
     vmem_spec = pl.BlockSpec(memory_space=pltpu.VMEM)
     dma = pltpu.SemaphoreType.DMA
     return pl.pallas_call(
-        functools.partial(kernel, n_dom, n_sub, cap, near, block, last_block, width),
+        functools.partial(kernel, n_dom, n_sub, cap, near, LEAD, block, last_block, width),
         out_shape=[pltpu.VMEM(displace.shape, f32)] * 2,
         in_specs=[any_spec] * 7,
         out_specs=[vmem_spec] * 2,

time: 47.7 us -> 46.1 us (0.966)
  Pallas kernels: 43.6 us -> 41.7 us
    pallas_call x1, Pallas kernels: 43.6 us -> 41.7 us  [body(): pl.pallas_call(functools.partial(kernel, n_dom, n_sub, cap, near, LEAD, b...]
where the time goes in v1:
time: 46.1 us; the launch traced here: 45.7 us
  Pallas kernels  41.7 us (90%)
  local copies, waits for them, and re-layouts  3.33 us (7%)
  between operations  0.64 us (1%)
    pallas_call x1, Pallas kernels, body(): pl.pallas_call(functools.partial(kernel, n_dom, n_sub, cap, near, LEAD, b...  41.7 us
    unnamed x2, local copies, waits for them, and re-layouts  3.33 us

profile of v1, /device:TPU:1, one launch (start us, length us, event | category | flops | bytes accessed | tf_op | source)
XLA Modules:
  0.0 45.7 jit_solution(1870025219643067353)
XLA Ops:
  0.6 41.7 %stamp.1 = (f32[3,2048,128]{2,1,0:T(8,128)S(1)}, f32[3,2048,128]{2,1,0:T(8,128)S(1)}) custom-call(s32[3,1,128]{2,1,0:T(1,128)} %bitcast.1, s32[3,128]{1,0:T(4,128)} %pair_hbm.1, f32[3,2048,128]{2,1,0:T(8,128)} %d_hbm.1, f32[3,2048,128]{2,1,0:T(8,128)} %v_hbm.1, f32[2048,128]{1,0:T(8,128)} %m_hbm.1, f32[2048,128]{1,0:T(8,128)} %k_hbm.1, f32[3,64,4,128]{3,2,1,0:T(4,128)} %die_hbm.1), custom_call_target="tpu_custom_call" | custom-call | tf_op jit(solution)/shard_map/stamp/pallas_call | solution.py:422
  42.3 1.7 %copy.11 = f32[3,2048,128]{2,1,0:T(8,128)} copy(f32[3,2048,128]{2,1,0:T(8,128)S(1)} %get-tuple-element.2) | data formatting | bytes 6291456
  44.0 1.7 %copy.12 = f32[3,2048,128]{2,1,0:T(8,128)} copy(f32[3,2048,128]{2,1,0:T(8,128)S(1)} %get-tuple-element.3) | data formatting | bytes 6291456

commit v2 on v0

--- a/solution.py
+++ b/solution.py
@@ -14,6 +14,8 @@
 MESH = pl.DeviceIdType.MESH
 PAD = 16
 HALO = 8
+CORES = 2
+LEAD = 1
 
 
 def next_col(x):
@@ -72,18 +74,18 @@
 
 
 def kernel(
-    n_dom, n_sub, cap, near, block, last_block, width,
+    n_dom, n_sub, cap, near, lead, block, last_block, width,
     own_hbm, pair_hbm, d_hbm, v_hbm, m_hbm, k_hbm, die_hbm,
     od_ref, ov_ref,
-    own_ref, pair_ref, d0, d1, d2, vel, cm, kq, w4, die, req, passed, asked, asked_rows, asked_s, idx, idx_s, answer, got, planes, first_patch, ghost, above_u, above_z,
-    load_sem, halo_send, halo_recv, req_send, req_recv, ans_send, ans_recv, small_sem, ghost_sem,
+    own_ref, pair_ref, d0, d1, d2, vel, cm, kq, w4, die_x, die_y, die_z, req, passed, asked, asked_rows, asked_s, idx, idx_s, answer, got, planes, first_patch, ghost, above_u, above_z,
+    load_sem, halo_send, halo_recv, die_send, die_recv, req_send, req_recv, ans_send, ans_recv, small_sem, ghost_sem,
 ):
     n = n_dom * n_sub
     steps, seg = pair_hbm.shape
     here = d_hbm.shape[1]
     stride = here // seg
     ncol = d_hbm.shape[2]
-    slots = steps * cap
+    assert steps == 3
     lists_rows = asked_s.shape[0]
     patches = die_hbm.shape[1]
     dom, sub = lax.axis_index("dom"), lax.axis_index("sub")
@@ -93,8 +95,10 @@
         return (lax.div(i, n_sub), lax.rem(i, n_sub))
 
     far = n // near
+    lines = (n_sub, far // n_sub, near // CORES)
     my_w = lax.rem(dom, near)
-    my_g = lax.div(dom, near) * n_sub + sub
+    my_x, my_y, my_z, my_core = sub, lax.div(dom, near), lax.div(my_w, CORES), lax.rem(my_w, CORES)
+    my_g = my_y * n_sub + my_x
 
     def device_at(g, w):
         return (lax.div(g, n_sub) * near + w, lax.rem(g, n_sub))
@@ -104,9 +108,6 @@
 
     def other_member(t):
         return lax.rem(my_w + t, near)
-
-    def partner(t):
-        return lax.rem(me + t * 37, n)
 
     following, previous = lax.rem(me + 1, n), lax.rem(me + n - 1, n)
 
@@ -120,7 +121,9 @@
         pltpu.make_async_copy(v_hbm, vel.at[:, inner], load_sem.at[1]),
         pltpu.make_async_copy(m_hbm, cm.at[inner], load_sem.at[2]),
         pltpu.make_async_copy(k_hbm, kq.at[inner], load_sem.at[3]),
-        pltpu.make_async_copy(die_hbm, die, load_sem.at[4]),
+        pltpu.make_async_copy(die_hbm.at[0], die_x.at[my_x], load_sem.at[4]),
+        pltpu.make_async_copy(die_hbm.at[1], die_y.at[my_y], load_sem.at[7]),
+        pltpu.make_async_copy(die_hbm.at[2], die_z.at[0], load_sem.at[8]),
     ]
     for copy in lists + loads:
         copy.start()
@@ -142,6 +145,21 @@
     lax.fori_loop(1, near, greet_members, 0)
     greet(device(following))
     greet(device(previous))
+
+    pl.semaphore_wait(barrier, far + near)
+
+    for axis, (count, mine, copies) in enumerate(zip(lines, (my_x, my_y, my_z), (die_x, die_y, die_z))):
+        for t in range(1, count):
+            there = lax.rem(mine + t, count)
+            to = (
+                device_at(my_y * n_sub + there, my_w),
+                device_at(there * n_sub + my_x, my_w),
+                device_at(my_g, there * CORES + my_core),
+            )[axis]
+            pltpu.make_async_remote_copy(
+                die_hbm.at[axis], copies.at[count - t if axis == 2 else mine],
+                die_send.at[axis], die_recv.at[axis], device_id=to, device_id_type=MESH,
+            ).start()
 
     lane_of = lax.broadcasted_iota(jnp.int32, (n, 128), 1)
     row = lax.broadcasted_iota(jnp.int32, (n, seg), 0)
@@ -157,15 +175,41 @@
         wide = jnp.broadcast_to(own, (seg, seg))
         same = (wide == wide.T) & before
         slot = jnp.minimum(jnp.sum(same.astype(jnp.int32), axis=0, keepdims=True), cap - 1)
-        places.append(own * slots + (s * cap + slot))
+        own_dom, own_x = lax.div(own, n_sub), lax.rem(own, n_sub)
+        own_y, own_w = lax.div(own_dom, near), lax.rem(own_dom, near)
+        own_z, own_core = lax.div(own_w, CORES), lax.rem(own_w, CORES)
+        line, at_line = (
+            (own_y * near + own_w, own_x),
+            (own_x * near + own_w, own_y),
+            ((own_y * n_sub + own_x) * CORES + own_core, lax.rem(own_z + (lines[2] - my_z), lines[2])),
+        )[s]
+        places.append((s * n + line * lines[s] + at_line) * cap + slot)
         pair = pair_ref[s : s + 1, :]
         mine = owner_of == own
         for k in range(cap):
             chosen = jnp.where(mine & (slot == k), pair, 0)
             table = jnp.where(lane_of == s * cap + k, jnp.sum(chosen, axis=1, keepdims=True), table)
-    req[...] = table.reshape(far, near, 128)
-    pl.semaphore_wait(barrier, far + near)
-
+    by_group = [table[near * g : near * (g + 1)] for g in range(far)]
+    lane = lax.broadcasted_iota(jnp.int32, (near, 128), 1)
+
+    def lanes_of(s, value, to):
+        value = jnp.where((lane >= s * cap) & (lane < (s + 1) * cap), value, 0)
+        shift = to - s * cap
+        return pltpu.roll(value, shift, 1) if shift else value
+
+    firsts = (0, lines[0] * cap, (lines[0] + lines[1]) * cap)
+    along_x = [
+        sum(lanes_of(0, by_group[y * n_sub + x], firsts[0] + x * cap) for x in range(lines[0])) for y in range(lines[1])
+    ]
+    along_y = [
+        sum(lanes_of(1, by_group[y * n_sub + x], firsts[1] + y * cap) for y in range(lines[1])) for x in range(lines[0])
+    ]
+    for g in range(far):
+        along_z = 0
+        for z in range(lines[2]):
+            turned = pltpu.roll(by_group[g], near - z * CORES, 0) if z else by_group[g]
+            along_z = along_z + lanes_of(2, turned, firsts[2] + z * cap)
+        req[g] = along_x[g // n_sub] + along_y[g % n_sub] + along_z
     def ask(t, carry):
         g = other_group(t)
         pltpu.make_async_remote_copy(
@@ -258,24 +302,61 @@
     to_scalar.wait()
     idx_copy.wait()
 
-    def gather(p, dst, at):
-        p_dom, p_sub = device(p)
-        w, g = lax.rem(p_dom, near), lax.div(p_dom, near) * n_sub + p_sub
-        for s in range(steps):
-            for k in range(cap):
-                dst[at + (s * cap + k)] = die[s, jnp.clip(asked_s[s * cap + k, w * far + g], 0, patches - 1)]
-
-    def reply(t, carry):
-        p = partner(t)
-        gather(p, answer, p * slots)
-        pltpu.make_async_remote_copy(
-            answer.at[pl.ds(p * slots, slots)], got.at[pl.ds(me * slots, slots)], ans_send, ans_recv,
-            device_id=device(p), device_id_type=MESH,
-        ).start()
-        return carry
-
-    lax.fori_loop(1, n, reply, 0)
-    gather(me, got, me * slots)
+    for axis, copies in enumerate((die_x, die_y, die_z)):
+        others = copies.at[pl.ds(0, lines[axis] - 1)]
+        pltpu.make_async_copy(others, others, die_recv.at[axis]).wait()
+
+    def gather(axis, w, g, dst, at):
+        copies = (die_x, die_y, die_z)[axis]
+        for i in range(lines[axis] * cap):
+            patch = jnp.clip(asked_s[firsts[axis] + i, w * far + g], 0, patches - 1)
+            dst[at + i] = copies[i // cap, patch]
+
+    def line_of(axis, y, x, w):
+        return (y * near + w, x * near + w, (y * n_sub + x) * CORES + lax.rem(w, CORES))[axis]
+
+    def planes_at(axis, y, x, w):
+        return (axis * n + line_of(axis, y, x, w) * lines[axis]) * cap
+
+    def reply(axis, y, x, w, wanted):
+        g = y * n_sub + x
+
+        @pl.when(wanted & ((g != my_g) | (w != my_w)))
+        def _():
+            size = lines[axis] * cap
+            there, here_at = planes_at(axis, y, x, w), planes_at(axis, my_y, my_x, my_w)
+            gather(axis, w, g, answer, there)
+            pltpu.make_async_remote_copy(
+                answer.at[pl.ds(there, size)], got.at[pl.ds(here_at, size)], ans_send, ans_recv,
+                device_id=device_at(g, w), device_id_type=MESH,
+            ).start()
+
+    rounds = lines[0] * CORES
+    assert lines[0] == lines[1]
+
+    def in_round(i):
+        return (i >= 0) & (i < rounds)
+
+    def reply_round(r, carry):
+        for layer in range(lines[2]):
+            i = r - lead * layer
+            at_y = lax.rem(my_y * CORES + my_core + 3 * (i + rounds), rounds)
+            at_x = lax.rem(my_x * CORES + my_core + 3 * (i + rounds), rounds)
+            w_y = layer * CORES + lax.rem(at_y, CORES)
+            w_x = layer * CORES + lax.rem(at_x, CORES)
+            reply(0, lax.div(at_y, CORES), my_x, w_y, in_round(i))
+            reply(1, my_y, lax.div(at_x, CORES), w_x, in_round(i))
+        i = r - lead * my_z
+        for part in range(lines[0]):
+            at = lax.rem(my_g * CORES + my_core + 13 * ((i + rounds) * lines[0] + part), far * CORES)
+            g = lax.div(at, CORES)
+            reply(2, lax.div(g, n_sub), lax.rem(g, n_sub), my_z * CORES + lax.rem(at, CORES), in_round(i))
+        return carry
+
+    assert lead * (lines[2] - 1) <= rounds
+    lax.fori_loop(0, rounds + lead * (lines[2] - 1), reply_round, 0)
+    for axis in range(3):
+        gather(axis, my_w, my_g, got, planes_at(axis, my_y, my_x, my_w))
 
     def free_step(src, d_to, v_to, first_row, count, size):
         def part(b, carry):
@@ -311,7 +392,7 @@
     free_step(d1, same_rows(d2), same_rows(vel), PAD - HALO, blocks, block)
     free_step(d2, own_rows(od_ref), own_rows(ov_ref), PAD, here // last_block, last_block)
 
-    wire = pl.ds(0, (n - 1) * slots)
+    wire = pl.ds(0, (3 * n - sum(lines)) * cap)
     pltpu.make_async_copy(answer.at[wire], got.at[wire], ans_recv).wait()
 
     for s in range(steps):
@@ -384,6 +465,9 @@
     lax.fori_loop(0, seg // width, correct_above, 0)
 
     pltpu.make_async_copy(answer.at[wire], got.at[wire], ans_send).wait()
+    for axis, copies in enumerate((die_x, die_y, die_z)):
+        others = copies.at[pl.ds(0, lines[axis] - 1)]
+        pltpu.make_async_copy(others, others, die_send.at[axis]).wait()
     pltpu.make_async_copy(req.at[pl.ds(0, far - 1)], passed.at[pl.ds(0, far - 1)], req_send.at[0]).wait()
     pltpu.make_async_copy(asked.at[pl.ds(0, near - 1)], asked.at[pl.ds(0, near - 1)], req_send.at[1]).wait()
 
@@ -393,7 +477,6 @@
     here, ncol = displace.shape[1:]
     steps, seg = pairs.shape
     cap = max(2, 2 * seg // n)
-    slots = steps * cap
     ext = here + 2 * PAD
     tiles = (here + 2 * HALO) // 8
     block = 8 * max(b for b in range(1, 44) if tiles % b == 0)
@@ -401,12 +484,13 @@
     width = min(32, seg)
     near = min(8, n_dom // 2)
     far = n // near
+    lanes = (n_sub + far // n_sub + near // CORES) * cap
     f32, i32 = jnp.float32, jnp.int32
     any_spec = pl.BlockSpec(memory_space=pl.ANY)
     vmem_spec = pl.BlockSpec(memory_space=pltpu.VMEM)
     dma = pltpu.SemaphoreType.DMA
     return pl.pallas_call(
-        functools.partial(kernel, n_dom, n_sub, cap, near, block, last_block, width),
+        functools.partial(kernel, n_dom, n_sub, cap, near, LEAD, block, last_block, width),
         out_shape=[pltpu.VMEM(displace.shape, f32)] * 2,
         in_specs=[any_spec] * 7,
         out_specs=[vmem_spec] * 2,
@@ -420,22 +504,24 @@
             pltpu.VMEM((ext, ncol), f32),
             pltpu.VMEM((ext, ncol), f32),
             pltpu.VMEM((ext, ncol), f32),
-            pltpu.VMEM(die_planes.shape, f32),
+            pltpu.VMEM((n_sub,) + die_planes.shape[1:], f32),
+            pltpu.VMEM((far // n_sub,) + die_planes.shape[1:], f32),
+            pltpu.VMEM((near // CORES,) + die_planes.shape[1:], f32),
             pltpu.VMEM((far, near, 128), i32),
             pltpu.VMEM((far, near, 128), i32),
             pltpu.VMEM((near, far, 128), i32),
-            pltpu.VMEM((-(-slots // 8) * 8, n), i32),
-            pltpu.SMEM((-(-slots // 8) * 8, n), i32),
+            pltpu.VMEM((-(-lanes // 8) * 8, n), i32),
+            pltpu.SMEM((-(-lanes // 8) * 8, n), i32),
             pltpu.VMEM((8, seg), i32),
             pltpu.SMEM((8, seg), i32),
-            pltpu.VMEM((n * slots, 4, ncol), f32),
-            pltpu.VMEM((n * slots, 4, ncol), f32),
+            pltpu.VMEM((n * steps * cap, 4, ncol), f32),
+            pltpu.VMEM((n * steps * cap, 4, ncol), f32),
             pltpu.VMEM((steps, seg * 4 + 32, ncol), f32),
             pltpu.VMEM((steps, 4, ncol), f32),
             pltpu.VMEM((steps, 4, ncol), f32),
             pltpu.VMEM((2, 3, seg + 8, ncol), f32),
             pltpu.VMEM((2, 3, seg + 8, ncol), f32),
-            dma((7,)), dma((8,)), dma((8,)), dma((2,)), dma((2,)), dma, dma, dma((2,)), dma((2,)),
+            dma((9,)), dma((8,)), dma((8,)), dma((3,)), dma((3,)), dma((2,)), dma((2,)), dma, dma, dma((2,)), dma((2,)),
         ],
         compiler_params=pltpu.CompilerParams(
             collective_id=0, has_side_effects=True, vmem_limit_bytes=40 * 1024 * 1024

time: 47.7 us -> 46.3 us (0.971)
  Pallas kernels: 43.6 us -> 42.2 us
    pallas_call x1, Pallas kernels: 43.6 us -> 42.2 us  [body(): pl.pallas_call(functools.partial(kernel, n_dom, n_sub, cap, near, LEAD, b...]
where the time goes in v2:
time: 46.3 us; the launch traced here: 46.2 us
  Pallas kernels  42.2 us (91%)
  local copies, waits for them, and re-layouts  3.33 us (7%)
  between operations  0.64 us (1%)
    pallas_call x1, Pallas kernels, body(): pl.pallas_call(functools.partial(kernel, n_dom, n_sub, cap, near, LEAD, b...  42.2 us
    unnamed x2, local copies, waits for them, and re-layouts  3.33 us

profile of v2, /device:TPU:1, one launch (start us, length us, event | category | flops | bytes accessed | tf_op | source)
XLA Modules:
  0.0 46.2 jit_solution(8151370773601498655)
XLA Ops:
  0.6 42.2 %stamp.1 = (f32[3,2048,128]{2,1,0:T(8,128)S(1)}, f32[3,2048,128]{2,1,0:T(8,128)S(1)}) custom-call(s32[3,1,128]{2,1,0:T(1,128)} %bitcast.1, s32[3,128]{1,0:T(4,128)} %pair_hbm.1, f32[3,2048,128]{2,1,0:T(8,128)} %d_hbm.1, f32[3,2048,128]{2,1,0:T(8,128)} %v_hbm.1, f32[2048,128]{1,0:T(8,128)} %m_hbm.1, f32[2048,128]{1,0:T(8,128)} %k_hbm.1, f32[3,64,4,128]{3,2,1,0:T(4,128)} %die_hbm.1), custom_call_target="tpu_custom_call" | custom-call | tf_op jit(solution)/shard_map/stamp/pallas_call | solution.py:492
  42.9 1.7 %copy.11 = f32[3,2048,128]{2,1,0:T(8,128)} copy(f32[3,2048,128]{2,1,0:T(8,128)S(1)} %get-tuple-element.2) | data formatting | bytes 6291456
  44.5 1.7 %copy.12 = f32[3,2048,128]{2,1,0:T(8,128)} copy(f32[3,2048,128]{2,1,0:T(8,128)S(1)} %get-tuple-element.3) | data formatting | bytes 6291456

commit v3 on v2

--- a/solution.py
+++ b/solution.py
@@ -77,7 +77,7 @@
     n_dom, n_sub, cap, near, lead, block, last_block, width,
     own_hbm, pair_hbm, d_hbm, v_hbm, m_hbm, k_hbm, die_hbm,
     od_ref, ov_ref,
-    own_ref, pair_ref, d0, d1, d2, vel, cm, kq, w4, die_x, die_y, die_z, req, passed, asked, asked_rows, asked_s, idx, idx_s, answer, got, planes, first_patch, ghost, above_u, above_z,
+    own_ref, pair_ref, d0, d1, d2, vel, cm, kq, w4, die_x, die_y, die_z, req, passed, asked, asked_rows, asked_s, idx, idx_s, answer, got, planes, first_patch, ghost, above_u, above_z, term,
     load_sem, halo_send, halo_recv, die_send, die_recv, req_send, req_recv, ans_send, ans_recv, small_sem, ghost_sem,
 ):
     n = n_dom * n_sub
@@ -295,8 +295,37 @@
 
     lax.fori_loop(0, blocks, weights, 0)
 
+    def free_step(src, d_to, v_to, first_row, count, size):
+        def part(b, carry):
+            base = pl.multiple_of(first_row + b * size, 8)
+            for i in range(size // 8 + 1):
+                at = pl.ds(base + 8 * (i - 1), 8)
+                below = pl.ds(base + 8 * (i - 1) + 1, 8)
+                for c in range(3):
+                    d = src[c, at, :]
+                    box = d + src[c, below, :]
+                    t = kq[at, :] * (box + next_col(box))
+                    term[c, 8 * i : 8 * (i + 1), :] = t
+                    if i:
+                        t = t + term[c, 8 * i - 1 : 8 * i + 7, :]
+                        force = t + prev_col(t) - w4[at, :] * d
+                        v = vel[c, at, :] + cm[at, :] * force
+                        v_to(base, size)[c, 8 * (i - 1) : 8 * i, :] = v
+                        d_to(base, size)[c, 8 * (i - 1) : 8 * i, :] = d + time_step * v
+            return carry
+
+        lax.fori_loop(0, count, part, 0)
+
+    def same_rows(ref):
+        return lambda base, size: ref.at[:, pl.ds(base, size)]
+
+    def own_rows(ref):
+        return lambda base, size: ref.at[:, pl.ds(pl.multiple_of(base - PAD, 8), size)]
+
+    free_step(d0, same_rows(d1), same_rows(vel), PAD - HALO, blocks, block)
+
     pltpu.make_async_copy(asked, asked, req_recv.at[1]).wait()
-    asked_rows[...] = asked[...].reshape(n, 128).T[:lists_rows]
+    asked_rows[...] = jnp.clip(asked[...].reshape(n, 128).T[:lists_rows], 0, patches - 1)
     to_scalar = pltpu.make_async_copy(asked_rows, asked_s, small_sem.at[1])
     to_scalar.start()
     to_scalar.wait()
@@ -309,8 +338,7 @@
     def gather(axis, w, g, dst, at):
         copies = (die_x, die_y, die_z)[axis]
         for i in range(lines[axis] * cap):
-            patch = jnp.clip(asked_s[firsts[axis] + i, w * far + g], 0, patches - 1)
-            dst[at + i] = copies[i // cap, patch]
+            dst[at + i] = copies[i // cap, asked_s[firsts[axis] + i, w * far + g]]
 
     def line_of(axis, y, x, w):
         return (y * near + w, x * near + w, (y * n_sub + x) * CORES + lax.rem(w, CORES))[axis]
@@ -358,37 +386,6 @@
     for axis in range(3):
         gather(axis, my_w, my_g, got, planes_at(axis, my_y, my_x, my_w))
 
-    def free_step(src, d_to, v_to, first_row, count, size):
-        def part(b, carry):
-            base = pl.multiple_of(first_row + b * size, 8)
-            top_row = lax.broadcasted_iota(jnp.int32, (8, ncol), 0) == 0
-            shifted = [None] * 3
-            for i in range(size // 8 + 1):
-                at = pl.ds(base + 8 * (i - 1), 8)
-                below = pl.ds(base + 8 * (i - 1) + 1, 8)
-                for c in range(3):
-                    d = src[c, at, :]
-                    box = d + src[c, below, :]
-                    t = kq[at, :] * (box + next_col(box))
-                    down = pltpu.roll(t, 1, 0)
-                    if i:
-                        t = t + jnp.where(top_row, shifted[c], down)
-                        force = t + prev_col(t) - w4[at, :] * d
-                        v = vel[c, at, :] + cm[at, :] * force
-                        v_to(base, size)[c, 8 * (i - 1) : 8 * i, :] = v
-                        d_to(base, size)[c, 8 * (i - 1) : 8 * i, :] = d + time_step * v
-                    shifted[c] = down
-            return carry
-
-        lax.fori_loop(0, count, part, 0)
-
-    def same_rows(ref):
-        return lambda base, size: ref.at[:, pl.ds(base, size)]
-
-    def own_rows(ref):
-        return lambda base, size: ref.at[:, pl.ds(pl.multiple_of(base - PAD, 8), size)]
-
-    free_step(d0, same_rows(d1), same_rows(vel), PAD - HALO, blocks, block)
     free_step(d1, same_rows(d2), same_rows(vel), PAD - HALO, blocks, block)
     free_step(d2, own_rows(od_ref), own_rows(ov_ref), PAD, here // last_block, last_block)
 
@@ -521,6 +518,7 @@
             pltpu.VMEM((steps, 4, ncol), f32),
             pltpu.VMEM((2, 3, seg + 8, ncol), f32),
             pltpu.VMEM((2, 3, seg + 8, ncol), f32),
+            pltpu.VMEM((3, max(block, last_block) + 8, ncol), f32),
             dma((9,)), dma((8,)), dma((8,)), dma((3,)), dma((3,)), dma((2,)), dma((2,)), dma, dma, dma((2,)), dma((2,)),
         ],
         compiler_params=pltpu.CompilerParams(

time: 46.3 us -> 45.3 us (0.978)
  Pallas kernels: 42.2 us -> 41.2 us
    pallas_call x1, Pallas kernels: 42.2 us -> 41.2 us  [body(): pl.pallas_call(functools.partial(kernel, n_dom, n_sub, cap, near, LEAD, b...]
where the time goes in v3:
time: 45.3 us; the launch traced here: 45.2 us
  Pallas kernels  41.2 us (91%)
  local copies, waits for them, and re-layouts  3.33 us (7%)
  between operations  0.64 us (1%)
    pallas_call x1, Pallas kernels, body(): pl.pallas_call(functools.partial(kernel, n_dom, n_sub, cap, near, LEAD, b...  41.2 us
    unnamed x2, local copies, waits for them, and re-layouts  3.33 us

profile of v3, /device:TPU:1, one launch (start us, length us, event | category | flops | bytes accessed | tf_op | source)
XLA Modules:
  0.0 45.2 jit_solution(9184391263794380525)
XLA Ops:
  0.6 41.2 %stamp.1 = (f32[3,2048,128]{2,1,0:T(8,128)S(1)}, f32[3,2048,128]{2,1,0:T(8,128)S(1)}) custom-call(s32[3,1,128]{2,1,0:T(1,128)} %bitcast.1, s32[3,128]{1,0:T(4,128)} %pair_hbm.1, f32[3,2048,128]{2,1,0:T(8,128)} %d_hbm.1, f32[3,2048,128]{2,1,0:T(8,128)} %v_hbm.1, f32[2048,128]{1,0:T(8,128)} %m_hbm.1, f32[2048,128]{1,0:T(8,128)} %k_hbm.1, f32[3,64,4,128]{3,2,1,0:T(4,128)} %die_hbm.1), custom_call_target="tpu_custom_call" | custom-call | tf_op jit(solution)/shard_map/stamp/pallas_call | solution.py:489
  41.9 1.7 %copy.11 = f32[3,2048,128]{2,1,0:T(8,128)} copy(f32[3,2048,128]{2,1,0:T(8,128)S(1)} %get-tuple-element.2) | data formatting | bytes 6291456
  43.5 1.7 %copy.12 = f32[3,2048,128]{2,1,0:T(8,128)} copy(f32[3,2048,128]{2,1,0:T(8,128)S(1)} %get-tuple-element.3) | data formatting | bytes 6291456

commit v4 on v3

--- a/solution.py
+++ b/solution.py
@@ -76,8 +76,8 @@
 def kernel(
     n_dom, n_sub, cap, near, lead, block, last_block, width,
     own_hbm, pair_hbm, d_hbm, v_hbm, m_hbm, k_hbm, die_hbm,
-    od_ref, ov_ref,
-    own_ref, pair_ref, d0, d1, d2, vel, cm, kq, w4, die_x, die_y, die_z, req, passed, asked, asked_rows, asked_s, idx, idx_s, answer, got, planes, first_patch, ghost, above_u, above_z, term,
+    od_ref, ov_ref, share_u, share_z,
+    own_ref, pair_ref, d0, d1, d2, vel, cm, kq, w4, die_x, die_y, die_z, req, passed, asked, asked_rows, asked_s, idx, idx_s, answer, got, planes, first_patch, ghost, term,
     load_sem, halo_send, halo_recv, die_send, die_recv, req_send, req_recv, ans_send, ans_recv, small_sem, ghost_sem,
 ):
     n = n_dom * n_sub
@@ -422,15 +422,11 @@
 
         nearby = [[planes[s, pl.ds(q * width * 4 + c, width, stride=4), :] for c in range(4)] for s in range(steps)]
         u, z = contact_response(nearby, rows)
-        for c in range(3):
-            for o in range(0, 3):
-                at = pl.ds(q * chunk + o, width, stride=stride)
-                od_ref[c, at, :] += u[o][c]
-                ov_ref[c, at, :] += z[o][c]
-            for o in (-2, -1):
-                at = pl.ds(pl.multiple_of(q * width, 8), width)
-                above_u[o + 2, c, at, :] = u[o][c]
-                above_z[o + 2, c, at, :] = z[o][c]
+        at = pl.ds(pl.multiple_of(q * width, 8), width)
+        for o in range(-2, 3):
+            for c in range(3):
+                share_u[o + 2, c, at, :] = u[o][c]
+                share_z[o + 2, c, at, :] = z[o][c]
         return carry
 
     lax.fori_loop(0, seg // width, correct, 0)
@@ -447,19 +443,8 @@
     u, z = contact_response(nearby, ghost_rows)
     for o in (-2, -1):
         for c in range(3):
-            above_u[o + 2, c, pl.ds(seg, 1), :] = u[o][c]
-            above_z[o + 2, c, pl.ds(seg, 1), :] = z[o][c]
-
-    def correct_above(q, carry):
-        for o in (-2, -1):
-            at = pl.ds(q * chunk + stride + o, width, stride=stride)
-            block_after = pl.ds(q * width + 1, width)
-            for c in range(3):
-                od_ref[c, at, :] += above_u[o + 2, c, block_after, :]
-                ov_ref[c, at, :] += above_z[o + 2, c, block_after, :]
-        return carry
-
-    lax.fori_loop(0, seg // width, correct_above, 0)
+            share_u[o + 2, c, pl.ds(seg, 1), :] = u[o][c]
+            share_z[o + 2, c, pl.ds(seg, 1), :] = z[o][c]
 
     pltpu.make_async_copy(answer.at[wire], got.at[wire], ans_send).wait()
     for axis, copies in enumerate((die_x, die_y, die_z)):
@@ -467,6 +452,29 @@
         pltpu.make_async_copy(others, others, die_send.at[axis]).wait()
     pltpu.make_async_copy(req.at[pl.ds(0, far - 1)], passed.at[pl.ds(0, far - 1)], req_send.at[0]).wait()
     pltpu.make_async_copy(asked.at[pl.ds(0, near - 1)], asked.at[pl.ds(0, near - 1)], req_send.at[1]).wait()
+
+
+def add_share(parts, stride, d_ref, v_ref, share_u, share_z, od_hbm, ov_hbm, d_sum, v_sum, sem):
+    here = d_ref.shape[1]
+    chunk = here // parts
+    width = chunk // stride
+    copies = []
+    for q in range(parts):
+        rows = pl.ds(q * chunk, chunk)
+        for a, (src, share, total, dst) in enumerate(
+            ((d_ref, share_u, d_sum, od_hbm), (v_ref, share_z, v_sum, ov_hbm))
+        ):
+            total[:, rows, :] = src[:, rows, :]
+            for o in range(-2, 3):
+                at = pl.ds(q * chunk + (o + stride if o < 0 else o), width, stride=stride)
+                block = pl.ds(q * width + (1 if o < 0 else 0), width)
+                for c in range(3):
+                    total[c, at, :] += share[o + 2, c, block, :]
+            copy = pltpu.make_async_copy(total.at[:, rows], dst.at[:, rows], sem.at[a, q])
+            copy.start()
+            copies.append(copy)
+    for copy in copies:
+        copy.wait()
 
 
 def body(n_dom, n_sub, displace, velocity, nodal_mass, stiffness, die_planes, owners, pairs):
@@ -486,11 +494,12 @@
     any_spec = pl.BlockSpec(memory_space=pl.ANY)
     vmem_spec = pl.BlockSpec(memory_space=pltpu.VMEM)
     dma = pltpu.SemaphoreType.DMA
-    return pl.pallas_call(
+    share = pltpu.VMEM((5, 3, seg + 8, ncol), f32)
+    results = pl.pallas_call(
         functools.partial(kernel, n_dom, n_sub, cap, near, LEAD, block, last_block, width),
-        out_shape=[pltpu.VMEM(displace.shape, f32)] * 2,
+        out_shape=[pltpu.VMEM(displace.shape, f32)] * 2 + [share] * 2,
         in_specs=[any_spec] * 7,
-        out_specs=[vmem_spec] * 2,
+        out_specs=[vmem_spec] * 4,
         scratch_shapes=[
             pltpu.VMEM((steps, 1, seg), i32),
             pltpu.VMEM((steps, seg), i32),
@@ -516,8 +525,6 @@
             pltpu.VMEM((steps, seg * 4 + 32, ncol), f32),
             pltpu.VMEM((steps, 4, ncol), f32),
             pltpu.VMEM((steps, 4, ncol), f32),
-            pltpu.VMEM((2, 3, seg + 8, ncol), f32),
-            pltpu.VMEM((2, 3, seg + 8, ncol), f32),
             pltpu.VMEM((3, max(block, last_block) + 8, ncol), f32),
             dma((9,)), dma((8,)), dma((8,)), dma((3,)), dma((3,)), dma((2,)), dma((2,)), dma, dma, dma((2,)), dma((2,)),
         ],
@@ -529,6 +536,16 @@
         pltpu.with_memory_space_constraint(x, pltpu.HBM)
         for x in (jnp.swapaxes(owners, 1, 2), pairs, displace, velocity, nodal_mass, stiffness, die_planes)
     ])
+    parts = 4
+    return pl.pallas_call(
+        functools.partial(add_share, parts, here // seg),
+        out_shape=[jax.ShapeDtypeStruct(displace.shape, f32)] * 2,
+        in_specs=[vmem_spec] * 4,
+        out_specs=[any_spec] * 2,
+        scratch_shapes=[pltpu.VMEM(displace.shape, f32), pltpu.VMEM(displace.shape, f32), dma((2, parts))],
+        compiler_params=pltpu.CompilerParams(vmem_limit_bytes=40 * 1024 * 1024),
+        name="add_share",
+    )(*[pltpu.with_memory_space_constraint(x, pltpu.VMEM) for x in results])
 
 
 def solution(mesh):

time: 45.3 us -> 43.9 us (0.969)
  local copies, waits for them, and re-layouts: 3.33 us -> 0 us
  Pallas kernels: 41.2 us -> 42.9 us
    unnamed x2 -> x0, local copies, waits for them, and re-layouts: 3.33 us -> none
    pallas_call x0 -> x1, Pallas kernels: none -> 2.94 us  [body(): pl.pallas_call(functools.partial(add_share, parts, here // seg), out_shap...]
    pallas_call x1, Pallas kernels: 41.2 us -> 40 us  [body(): pl.pallas_call(functools.partial(kernel, n_dom, n_sub, cap, near, LEAD, b...]
where the time goes in v4:
time: 43.9 us; the launch traced here: 43.6 us
  Pallas kernels  42.9 us (98%)
  between operations  0.64 us (1%)
    pallas_call x1, Pallas kernels, body(): pl.pallas_call(functools.partial(kernel, n_dom, n_sub, cap, near, LEAD, b...  40 us
    pallas_call x1, Pallas kernels, body(): pl.pallas_call(functools.partial(add_share, parts, here // seg), out_shap...  2.94 us

profile of v4, /device:TPU:1, one launch (start us, length us, event | category | flops | bytes accessed | tf_op | source)
XLA Modules:
  0.0 43.6 jit_solution(6117114494228323583)
XLA Ops:
  0.6 40.0 %stamp.1 = (f32[3,2048,128]{2,1,0:T(8,128)S(1)}, f32[3,2048,128]{2,1,0:T(8,128)S(1)}, f32[5,3,136,128]{3,2,1,0:T(8,128)S(1)}, f32[5,3,136,128]{3,2,1,0:T(8,128)S(1)}) custom-call(s32[3,1,128]{2,1,0:T(1,128)} %bitcast.1, s32[3,128]{1,0:T(4,128)} %pair_hbm.1, f32[3,2048,128]{2,1,0:T(8,128)} %d_hbm.1, f32[3,2048,128]{2,1,0:T(8,128)} %v_hbm.1, ...), custom_call_target="tpu_custom_call" | custom-call | tf_op jit(solution)/shard_map/stamp/pallas_call | solution.py:498
  40.7 2.9 %add_share.1 = (f32[3,2048,128]{2,1,0:T(8,128)}, f32[3,2048,128]{2,1,0:T(8,128)}) custom-call(f32[3,2048,128]{2,1,0:T(8,128)S(1)} %get-tuple-element.6.d_ref, f32[3,2048,128]{2,1,0:T(8,128)S(1)} %get-tuple-element.7.v_ref, f32[5,3,136,128]{3,2,1,0:T(8,128)S(1)} %get-tuple-element.8.share_u, f32[5,3,136,128]{3,2,1,0:T(8,128)S(1)} %get-tuple-element.9.share_z), custom_call_target="tpu_custom_call" | custom-call | tf_op jit(solution)/shard_map/add_share/pallas_call | solution.py:540

commit v5 on v4

--- a/solution.py
+++ b/solution.py
@@ -148,18 +148,49 @@
 
     pl.semaphore_wait(barrier, far + near)
 
-    for axis, (count, mine, copies) in enumerate(zip(lines, (my_x, my_y, my_z), (die_x, die_y, die_z))):
-        for t in range(1, count):
-            there = lax.rem(mine + t, count)
-            to = (
-                device_at(my_y * n_sub + there, my_w),
-                device_at(there * n_sub + my_x, my_w),
-                device_at(my_g, there * CORES + my_core),
-            )[axis]
-            pltpu.make_async_remote_copy(
-                die_hbm.at[axis], copies.at[count - t if axis == 2 else mine],
-                die_send.at[axis], die_recv.at[axis], device_id=to, device_id_type=MESH,
-            ).start()
+    sets = (die_x, die_y, die_z)
+    half = patches // 2
+
+    def along(axis, t):
+        return lax.rem((my_x, my_y, my_z)[axis] + t, lines[axis])
+
+    def device_along(axis, t):
+        there = along(axis, t)
+        return (
+            device_at(my_y * n_sub + there, my_w),
+            device_at(there * n_sub + my_x, my_w),
+            device_at(my_g, there * CORES + my_core),
+        )[axis]
+
+    def set_of(axis, t, seen):
+        return (t - seen) % lines[axis] if axis == 2 else along(axis, t)
+
+    def set_copy(axis, t, to, src, rows, number):
+        place = sets[axis].at[set_of(axis, t, to), rows]
+        return pltpu.make_async_remote_copy(
+            src, place, die_send.at[axis, number], die_recv.at[axis, number],
+            device_id=device_along(axis, to), device_id_type=MESH,
+        )
+
+    first_legs, second_legs = [], []
+    every = pl.ds(0, patches)
+    for axis, count in enumerate(lines):
+        assert count in (2, 4)
+        for number, to in enumerate((1, count - 1)[: count - 2 or 1]):
+            copy = set_copy(axis, 0, to, die_hbm.at[axis], every, number)
+            copy.start()
+            first_legs.append(copy)
+
+    def hand_sets_on():
+        for copy in first_legs:
+            copy.wait_recv()
+        for axis, count in enumerate(lines):
+            if count == 4:
+                for number, (came, to, rows) in enumerate(((3, 1, pl.ds(0, half)), (1, 3, pl.ds(half, half)))):
+                    src = sets[axis].at[set_of(axis, came, 0), rows]
+                    copy = set_copy(axis, came, to, src, rows, 2 + number)
+                    copy.start()
+                    second_legs.append(copy)
 
     lane_of = lax.broadcasted_iota(jnp.int32, (n, 128), 1)
     row = lax.broadcasted_iota(jnp.int32, (n, seg), 0)
@@ -268,6 +299,7 @@
 
     lax.fori_loop(1, near, hand_on, 0)
     pltpu.make_async_copy(passed.at[:, my_w], asked.at[my_w], req_recv.at[1]).start()
+    hand_sets_on()
 
     for copy in halos:
         copy.wait()
@@ -331,9 +363,8 @@
     to_scalar.wait()
     idx_copy.wait()
 
-    for axis, copies in enumerate((die_x, die_y, die_z)):
-        others = copies.at[pl.ds(0, lines[axis] - 1)]
-        pltpu.make_async_copy(others, others, die_recv.at[axis]).wait()
+    for copy in second_legs:
+        copy.wait_recv()
 
     def gather(axis, w, g, dst, at):
         copies = (die_x, die_y, die_z)[axis]
@@ -447,9 +478,8 @@
             share_z[o + 2, c, pl.ds(seg, 1), :] = z[o][c]
 
     pltpu.make_async_copy(answer.at[wire], got.at[wire], ans_send).wait()
-    for axis, copies in enumerate((die_x, die_y, die_z)):
-        others = copies.at[pl.ds(0, lines[axis] - 1)]
-        pltpu.make_async_copy(others, others, die_send.at[axis]).wait()
+    for copy in first_legs + second_legs:
+        copy.wait_send()
     pltpu.make_async_copy(req.at[pl.ds(0, far - 1)], passed.at[pl.ds(0, far - 1)], req_send.at[0]).wait()
     pltpu.make_async_copy(asked.at[pl.ds(0, near - 1)], asked.at[pl.ds(0, near - 1)], req_send.at[1]).wait()
 
@@ -526,7 +556,7 @@
             pltpu.VMEM((steps, 4, ncol), f32),
             pltpu.VMEM((steps, 4, ncol), f32),
             pltpu.VMEM((3, max(block, last_block) + 8, ncol), f32),
-            dma((9,)), dma((8,)), dma((8,)), dma((3,)), dma((3,)), dma((2,)), dma((2,)), dma, dma, dma((2,)), dma((2,)),
+            dma((9,)), dma((8,)), dma((8,)), dma((3, 4)), dma((3, 4)), dma((2,)), dma((2,)), dma, dma, dma((2,)), dma((2,)),
         ],
         compiler_params=pltpu.CompilerParams(
             collective_id=0, has_side_effects=True, vmem_limit_bytes=40 * 1024 * 1024

time: 43.9 us -> 41.4 us (0.943)
  Pallas kernels: 42.9 us -> 40.4 us
    pallas_call x1, Pallas kernels: 40 us -> 37.4 us  [body(): pl.pallas_call(functools.partial(kernel, n_dom, n_sub, cap, near, LEAD, b...]
where the time goes in v5:
time: 41.4 us; the launch traced here: 41 us
  Pallas kernels  40.4 us (98%)
  between operations  0.64 us (2%)
    pallas_call x1, Pallas kernels, body(): pl.pallas_call(functools.partial(kernel, n_dom, n_sub, cap, near, LEAD, b...  37.4 us
    pallas_call x1, Pallas kernels, body(): pl.pallas_call(functools.partial(add_share, parts, here // seg), out_shap...  2.94 us

profile of v5, /device:TPU:1, one launch (start us, length us, event | category | flops | bytes accessed | tf_op | source)
XLA Modules:
  0.0 41.0 jit_solution(4986255998620566150)
XLA Ops:
  0.6 37.4 %stamp.1 = (f32[3,2048,128]{2,1,0:T(8,128)S(1)}, f32[3,2048,128]{2,1,0:T(8,128)S(1)}, f32[5,3,136,128]{3,2,1,0:T(8,128)S(1)}, f32[5,3,136,128]{3,2,1,0:T(8,128)S(1)}) custom-call(s32[3,1,128]{2,1,0:T(1,128)} %bitcast.1, s32[3,128]{1,0:T(4,128)} %pair_hbm.1, f32[3,2048,128]{2,1,0:T(8,128)} %d_hbm.1, f32[3,2048,128]{2,1,0:T(8,128)} %v_hbm.1, ...), custom_call_target="tpu_custom_call" | custom-call | tf_op jit(solution)/shard_map/stamp/pallas_call | solution.py:528
  38.1 2.9 %add_share.1 = (f32[3,2048,128]{2,1,0:T(8,128)}, f32[3,2048,128]{2,1,0:T(8,128)}) custom-call(f32[3,2048,128]{2,1,0:T(8,128)S(1)} %get-tuple-element.6.d_ref, f32[3,2048,128]{2,1,0:T(8,128)S(1)} %get-tuple-element.7.v_ref, f32[5,3,136,128]{3,2,1,0:T(8,128)S(1)} %get-tuple-element.8.share_u, f32[5,3,136,128]{3,2,1,0:T(8,128)S(1)} %get-tuple-element.9.share_z), custom_call_target="tpu_custom_call" | custom-call | tf_op jit(solution)/shard_map/add_share/pallas_call | solution.py:570

commit v6 on v5

--- a/solution.py
+++ b/solution.py
@@ -333,15 +333,18 @@
             for i in range(size // 8 + 1):
                 at = pl.ds(base + 8 * (i - 1), 8)
                 below = pl.ds(base + 8 * (i - 1) + 1, 8)
+                k_here = kq[at, :]
+                if i:
+                    w_here, cm_here = w4[at, :], cm[at, :]
                 for c in range(3):
                     d = src[c, at, :]
                     box = d + src[c, below, :]
-                    t = kq[at, :] * (box + next_col(box))
+                    t = k_here * (box + next_col(box))
                     term[c, 8 * i : 8 * (i + 1), :] = t
                     if i:
                         t = t + term[c, 8 * i - 1 : 8 * i + 7, :]
-                        force = t + prev_col(t) - w4[at, :] * d
-                        v = vel[c, at, :] + cm[at, :] * force
+                        force = t + prev_col(t) - w_here * d
+                        v = vel[c, at, :] + cm_here * force
                         v_to(base, size)[c, 8 * (i - 1) : 8 * i, :] = v
                         d_to(base, size)[c, 8 * (i - 1) : 8 * i, :] = d + time_step * v
             return carry
@@ -354,12 +357,14 @@
     def own_rows(ref):
         return lambda base, size: ref.at[:, pl.ds(pl.multiple_of(base - PAD, 8), size)]
 
-    free_step(d0, same_rows(d1), same_rows(vel), PAD - HALO, blocks, block)
+    part_one = blocks // 2
+    free_step(d0, same_rows(d1), same_rows(vel), PAD - HALO, part_one, block)
 
     pltpu.make_async_copy(asked, asked, req_recv.at[1]).wait()
     asked_rows[...] = jnp.clip(asked[...].reshape(n, 128).T[:lists_rows], 0, patches - 1)
     to_scalar = pltpu.make_async_copy(asked_rows, asked_s, small_sem.at[1])
     to_scalar.start()
+    free_step(d0, same_rows(d1), same_rows(vel), PAD - HALO + part_one * block, blocks - part_one, block)
     to_scalar.wait()
     idx_copy.wait()
 
@@ -566,7 +571,7 @@
         pltpu.with_memory_space_constraint(x, pltpu.HBM)
         for x in (jnp.swapaxes(owners, 1, 2), pairs, displace, velocity, nodal_mass, stiffness, die_planes)
     ])
-    parts = 4
+    parts = 8 if seg >= 64 else 2
     return pl.pallas_call(
         functools.partial(add_share, parts, here // seg),
         out_shape=[jax.ShapeDtypeStruct(displace.shape, f32)] * 2,

time: 41.4 us -> 43 us (1.039)
  Pallas kernels: 40.4 us -> 42.2 us
    pallas_call x1, Pallas kernels: 37.4 us -> 39.4 us  [body(): pl.pallas_call(functools.partial(kernel, n_dom, n_sub, cap, near, LEAD, b...]
where the time goes in v6:
time: 43 us; the launch traced here: 42.9 us
  Pallas kernels  42.2 us (98%)
  between operations  0.64 us (1%)
    pallas_call x1, Pallas kernels, body(): pl.pallas_call(functools.partial(kernel, n_dom, n_sub, cap, near, LEAD, b...  39.4 us
    pallas_call x1, Pallas kernels, body(): pl.pallas_call(functools.partial(add_share, parts, here // seg), out_shap...  2.88 us

profile of v6, /device:TPU:1, one launch (start us, length us, event | category | flops | bytes accessed | tf_op | source)
XLA Modules:
  0.0 42.9 jit_solution(310922374062317394)
XLA Ops:
  0.6 39.4 %stamp.1 = (f32[3,2048,128]{2,1,0:T(8,128)S(1)}, f32[3,2048,128]{2,1,0:T(8,128)S(1)}, f32[5,3,136,128]{3,2,1,0:T(8,128)S(1)}, f32[5,3,136,128]{3,2,1,0:T(8,128)S(1)}) custom-call(s32[3,1,128]{2,1,0:T(1,128)} %bitcast.1, s32[3,128]{1,0:T(4,128)} %pair_hbm.1, f32[3,2048,128]{2,1,0:T(8,128)} %d_hbm.1, f32[3,2048,128]{2,1,0:T(8,128)} %v_hbm.1, ...), custom_call_target="tpu_custom_call" | custom-call | tf_op jit(solution)/shard_map/stamp/pallas_call | solution.py:533
  40.0 2.9 %add_share.1 = (f32[3,2048,128]{2,1,0:T(8,128)}, f32[3,2048,128]{2,1,0:T(8,128)}) custom-call(f32[3,2048,128]{2,1,0:T(8,128)S(1)} %get-tuple-element.6.d_ref, f32[3,2048,128]{2,1,0:T(8,128)S(1)} %get-tuple-element.7.v_ref, f32[5,3,136,128]{3,2,1,0:T(8,128)S(1)} %get-tuple-element.8.share_u, f32[5,3,136,128]{3,2,1,0:T(8,128)S(1)} %get-tuple-element.9.share_z), custom_call_target="tpu_custom_call" | custom-call | tf_op jit(solution)/shard_map/add_share/pallas_call | solution.py:575

commit v7 on v5

--- a/solution.py
+++ b/solution.py
@@ -174,12 +174,16 @@
 
     first_legs, second_legs = [], []
     every = pl.ds(0, patches)
-    for axis, count in enumerate(lines):
+
+    def send_set(axis):
+        count = lines[axis]
         assert count in (2, 4)
         for number, to in enumerate((1, count - 1)[: count - 2 or 1]):
             copy = set_copy(axis, 0, to, die_hbm.at[axis], every, number)
             copy.start()
             first_legs.append(copy)
+
+    send_set(2)
 
     def hand_sets_on():
         for copy in first_legs:
@@ -250,6 +254,8 @@
         return carry
 
     lax.fori_loop(1, far, ask, 0)
+    send_set(0)
+    send_set(1)
     pltpu.make_async_copy(req.at[my_g], passed.at[my_g], req_recv.at[0]).start()
 
     for s in range(steps):
@@ -566,7 +572,7 @@
         pltpu.with_memory_space_constraint(x, pltpu.HBM)
         for x in (jnp.swapaxes(owners, 1, 2), pairs, displace, velocity, nodal_mass, stiffness, die_planes)
     ])
-    parts = 4
+    parts = 8 if seg >= 64 else 2
     return pl.pallas_call(
         functools.partial(add_share, parts, here // seg),
         out_shape=[jax.ShapeDtypeStruct(displace.shape, f32)] * 2,

time: 41.4 us -> 41 us (level)
  no operation moved by 1% of the time
where the time goes in v7:
time: 41 us; the launch traced here: 40.8 us
  Pallas kernels  40.2 us (98%)
  between operations  0.64 us (2%)
    pallas_call x1, Pallas kernels, body(): pl.pallas_call(functools.partial(kernel, n_dom, n_sub, cap, near, LEAD, b...  37.3 us
    pallas_call x1, Pallas kernels, body(): pl.pallas_call(functools.partial(add_share, parts, here // seg), out_shap...  2.88 us

profile of v7, /device:TPU:1, one launch (start us, length us, event | category | flops | bytes accessed | tf_op | source)
XLA Modules:
  0.0 40.8 jit_solution(17099506135970337937)
XLA Ops:
  0.6 37.3 %stamp.1 = (f32[3,2048,128]{2,1,0:T(8,128)S(1)}, f32[3,2048,128]{2,1,0:T(8,128)S(1)}, f32[5,3,136,128]{3,2,1,0:T(8,128)S(1)}, f32[5,3,136,128]{3,2,1,0:T(8,128)S(1)}) custom-call(s32[3,1,128]{2,1,0:T(1,128)} %bitcast.1, s32[3,128]{1,0:T(4,128)} %pair_hbm.1, f32[3,2048,128]{2,1,0:T(8,128)} %d_hbm.1, f32[3,2048,128]{2,1,0:T(8,128)} %v_hbm.1, ...), custom_call_target="tpu_custom_call" | custom-call | tf_op jit(solution)/shard_map/stamp/pallas_call | solution.py:534
  37.9 2.9 %add_share.1 = (f32[3,2048,128]{2,1,0:T(8,128)}, f32[3,2048,128]{2,1,0:T(8,128)}) custom-call(f32[3,2048,128]{2,1,0:T(8,128)S(1)} %get-tuple-element.6.d_ref, f32[3,2048,128]{2,1,0:T(8,128)S(1)} %get-tuple-element.7.v_ref, f32[5,3,136,128]{3,2,1,0:T(8,128)S(1)} %get-tuple-element.8.share_u, f32[5,3,136,128]{3,2,1,0:T(8,128)S(1)} %get-tuple-element.9.share_z), custom_call_target="tpu_custom_call" | custom-call | tf_op jit(solution)/shard_map/add_share/pallas_call | solution.py:576

commit v8 on v7

--- a/solution.py
+++ b/solution.py
@@ -184,12 +184,13 @@
             first_legs.append(copy)
 
     send_set(2)
-
-    def hand_sets_on():
-        for copy in first_legs:
+    z_legs = len(first_legs)
+
+    def hand_sets_on(axes, arrived):
+        for copy in arrived:
             copy.wait_recv()
-        for axis, count in enumerate(lines):
-            if count == 4:
+        for axis in axes:
+            if lines[axis] == 4:
                 for number, (came, to, rows) in enumerate(((3, 1, pl.ds(0, half)), (1, 3, pl.ds(half, half)))):
                     src = sets[axis].at[set_of(axis, came, 0), rows]
                     copy = set_copy(axis, came, to, src, rows, 2 + number)
@@ -202,6 +203,9 @@
     owner_of = (lax.div(row_g, n_sub) * near + row_w) * n_sub + lax.rem(row_g, n_sub)
     before = lax.broadcasted_iota(jnp.int32, (seg, seg), 0) < lax.broadcasted_iota(jnp.int32, (seg, seg), 1)
     table = jnp.zeros((n, 128), jnp.int32)
+    bits = (patches - 1).bit_length()
+    in_word = 30 // bits
+    words = [None] * -(-steps * cap // in_word)
     places = []
     for copy in lists:
         copy.wait()
@@ -222,8 +226,14 @@
         pair = pair_ref[s : s + 1, :]
         mine = owner_of == own
         for k in range(cap):
-            chosen = jnp.where(mine & (slot == k), pair, 0)
-            table = jnp.where(lane_of == s * cap + k, jnp.sum(chosen, axis=1, keepdims=True), table)
+            word, at = divmod(s * cap + k, in_word)
+            chosen = jnp.where(mine & (slot == k), pair * (1 << (bits * at)), 0)
+            words[word] = chosen if words[word] is None else words[word] + chosen
+    for word, value in enumerate(words):
+        total = jnp.sum(value, axis=1, keepdims=True)
+        for at in range(min(in_word, steps * cap - word * in_word)):
+            field = (total >> (bits * at)) & ((1 << bits) - 1)
+            table = jnp.where(lane_of == word * in_word + at, field, table)
     by_group = [table[near * g : near * (g + 1)] for g in range(far)]
     lane = lax.broadcasted_iota(jnp.int32, (near, 128), 1)
 
@@ -293,6 +303,8 @@
 
     lax.fori_loop(0, here // last_block, prepare_block, 0)
 
+    hand_sets_on((2,), first_legs[:z_legs])
+
     pltpu.make_async_copy(req, passed, req_recv.at[0]).wait()
 
     def hand_on(t, carry):
@@ -305,7 +317,7 @@
 
     lax.fori_loop(1, near, hand_on, 0)
     pltpu.make_async_copy(passed.at[:, my_w], asked.at[my_w], req_recv.at[1]).start()
-    hand_sets_on()
+    hand_sets_on((0, 1), first_legs[z_legs:])
 
     for copy in halos:
         copy.wait()

time: 41 us -> 40.8 us (level)
  no operation moved by 1% of the time
where the time goes in v8:
time: 40.8 us; the launch traced here: 40.7 us
  Pallas kernels  40.1 us (98%)
  between operations  0.64 us (2%)
    pallas_call x1, Pallas kernels, body(): pl.pallas_call(functools.partial(kernel, n_dom, n_sub, cap, near, LEAD, b...  37.2 us
    pallas_call x1, Pallas kernels, body(): pl.pallas_call(functools.partial(add_share, parts, here // seg), out_shap...  2.88 us

profile of v8, /device:TPU:1, one launch (start us, length us, event | category | flops | bytes accessed | tf_op | source)
XLA Modules:
  0.0 40.7 jit_solution(6273631694593086318)
XLA Ops:
  0.6 37.2 %stamp.1 = (f32[3,2048,128]{2,1,0:T(8,128)S(1)}, f32[3,2048,128]{2,1,0:T(8,128)S(1)}, f32[5,3,136,128]{3,2,1,0:T(8,128)S(1)}, f32[5,3,136,128]{3,2,1,0:T(8,128)S(1)}) custom-call(s32[3,1,128]{2,1,0:T(1,128)} %bitcast.1, s32[3,128]{1,0:T(4,128)} %pair_hbm.1, f32[3,2048,128]{2,1,0:T(8,128)} %d_hbm.1, f32[3,2048,128]{2,1,0:T(8,128)} %v_hbm.1, ...), custom_call_target="tpu_custom_call" | custom-call | tf_op jit(solution)/shard_map/stamp/pallas_call | solution.py:546
  37.8 2.9 %add_share.1 = (f32[3,2048,128]{2,1,0:T(8,128)}, f32[3,2048,128]{2,1,0:T(8,128)}) custom-call(f32[3,2048,128]{2,1,0:T(8,128)S(1)} %get-tuple-element.6.d_ref, f32[3,2048,128]{2,1,0:T(8,128)S(1)} %get-tuple-element.7.v_ref, f32[5,3,136,128]{3,2,1,0:T(8,128)S(1)} %get-tuple-element.8.share_u, f32[5,3,136,128]{3,2,1,0:T(8,128)S(1)} %get-tuple-element.9.share_z), custom_call_target="tpu_custom_call" | custom-call | tf_op jit(solution)/shard_map/add_share/pallas_call | solution.py:588
